TPU v7x, 128 devices: a whole 4x4x4 slice. The times are simulated.
128 devices in a mesh: dp: 16 (over x_lo, z, core), tensor: 8 (over y, x_hi).
Axes of the slice: x: 4 (x_hi: 2, x_lo: 2; x = x_hi * 2 + x_lo), y: 4, z: 4, core: 2. Of those that a mesh axis runs over, the one named last changes fastest.
Arguments:
- tokens: bfloat16 [16384, 1024], P(('dp', 'tensor')), may hold values from -6 to 6
- lengths: int32 [16, 3], P('dp'), may hold values from 1 to 960, 1024 in all within a row
- qkv_weight: bfloat16 [2, 1024, 3, 1024], P(None, 'dp', None, 'tensor'), may hold values from -0.1875 to 0.1875
- qkv_bias: bfloat16 [2, 3, 1024], P(None, None, 'tensor'), may hold values from -3 to 3
- dense_weight: bfloat16 [2, 1024, 1024], P(None, 'tensor', 'dp'), may hold values from -0.75 to 0.75
- dense_bias: bfloat16 [2, 1024], replicated, may hold values from -2 to 2
- fc_in_weight: bfloat16 [2, 1024, 4096], P(None, 'dp', 'tensor'), may hold values from -0.1875 to 0.1875
- fc_in_bias: bfloat16 [2, 4096], P(None, 'tensor'), may hold values from -3 to 3
- fc_out_weight: bfloat16 [2, 4096, 1024], P(None, 'tensor', 'dp'), may hold values from -0.09375 to 0.09375
- fc_out_bias: bfloat16 [2, 1024], replicated, may hold values from -2 to 2
- norm_gain: bfloat16 [2, 2, 1024], replicated, may hold values from 0.5 to 1.5
- norm_bias: bfloat16 [2, 2, 1024], replicated, may hold values from -2 to 2
- cotangent: bfloat16 [16384, 1024], P(('dp', 'tensor')), may hold values from -6 to 6
Outputs:
- output: bfloat16 [16384, 1024], P(('dp', 'tensor'))
- input_grad: float32 [16384, 1024], P(('dp', 'tensor'))
- qkv_weight_grad: float32 [2, 1024, 3, 1024], P(None, 'dp', None, 'tensor')
- qkv_bias_grad: float32 [2, 3, 1024], P(None, None, 'tensor')
- dense_weight_grad: float32 [2, 1024, 1024], P(None, 'tensor', 'dp')
- dense_bias_grad: float32 [2, 1024], replicated
- fc_in_weight_grad: float32 [2, 1024, 4096], P(None, 'dp', 'tensor')
- fc_in_bias_grad: float32 [2, 4096], P(None, 'tensor')
- fc_out_weight_grad: float32 [2, 4096, 1024], P(None, 'tensor', 'dp')
- fc_out_bias_grad: float32 [2, 1024], replicated
- norm_gain_grad: float32 [2, 2, 1024], replicated
- norm_bias_grad: float32 [2, 2, 1024], replicated
Inputs may be any that keep to these rules, and one draw needn't show every extreme that they name: Each row of lengths holds 3 positive lengths that sum to 1024; the largest of each row is exactly 960.
All inputs are finite; a program needn't handle non-finite values.
Results may differ from a plain program's by a relative error of at most 0.023.
Values may be sent and summed in bfloat16 or wider, within the bound.
A program may use at most 192 MiB of HBM per device.

v0:
```python
from functools import partial

import jax
import jax.numpy as jnp
from jax import lax
from jax.sharding import PartitionSpec as P

HEAD_DIM = 64
ROT = 16


EPSILON = 1e-05
MASKED = -1000000000.0


def layer_norm(stream, scale_gain, shift_bias):
    average = jnp.mean(stream, axis=-1, keepdims=True)
    centered = stream - average
    spread = jnp.mean(centered * centered, axis=-1, keepdims=True)
    return centered * lax.rsqrt(spread + EPSILON) * scale_gain + shift_bias


def rotate(vectors, cosine, sine_table):
    half_rot = cosine.shape[-1]
    first_rot = vectors[..., :half_rot]
    second = vectors[..., half_rot : 2 * half_rot]
    untouched = vectors[..., 2 * half_rot :]
    return jnp.concatenate(
        [
            first_rot * cosine - second * sine_table,
            second * cosine + first_rot * sine_table,
            untouched,
        ],
        axis=-1,
    )


def positions(lengths, group_rows):
    endings = jnp.cumsum(lengths)
    starts = endings - lengths
    row_ids = jnp.arange(group_rows, dtype=jnp.int32)
    member = (row_ids[:, None] >= starts[None, :]) & (row_ids[:, None] < endings[None, :])
    numbers = jnp.arange(lengths.shape[0], dtype=jnp.int32)
    segment = jnp.sum(jnp.where(member, numbers[None, :], 0), axis=1)
    opening = jnp.sum(jnp.where(member, starts[None, :], 0), axis=1)
    return (segment, row_ids - opening)


def visible(segment, block_start, block_rows):
    group_rows = segment.shape[0]
    query_ids = block_start + jnp.arange(block_rows, dtype=jnp.int32)
    key_ids = jnp.arange(group_rows, dtype=jnp.int32)
    same_doc = segment[block_start : block_start + block_rows][:, None] == segment[None, :]
    return same_doc & (key_ids[None, :] <= query_ids[:, None])


def block_scores(block_queries, keys_rot, segment, block_start, block_rows, score_scale):
    scores = (
        jnp.einsum("bhe,khe->hbk", block_queries, keys_rot, preferred_element_type=jnp.float32)
        * score_scale
    )
    return jnp.where(visible(segment, block_start, block_rows)[None], scores, MASKED)


def attend(queries, keys_rot, values_in, segment, block_rows, score_scale):
    group_rows = queries.shape[0]
    outputs = []
    log_totals = []
    for block_start in range(0, group_rows, block_rows):
        block_queries = queries[block_start : block_start + block_rows]
        scores = block_scores(
            block_queries, keys_rot, segment, block_start, block_rows, score_scale
        )
        row_max = jnp.max(scores, axis=-1, keepdims=True)
        exponent = jnp.exp(scores - row_max)
        row_total = jnp.sum(exponent, axis=-1, keepdims=True)
        probability = (exponent / row_total).astype(jnp.bfloat16)
        outputs.append(
            jnp.einsum("hbk,khe->bhe", probability, values_in, preferred_element_type=jnp.float32)
        )
        log_totals.append(row_max + jnp.log(row_total))
    return (jnp.concatenate(outputs, axis=0), log_totals)


def attend_back(
    queries, keys_rot, values_in, log_totals, attended_grad, segment, block_rows, score_scale
):
    group_rows = queries.shape[0]
    keys_grad = jnp.zeros(keys_rot.shape, jnp.float32)
    values_grad = jnp.zeros(values_in.shape, jnp.float32)
    query_parts = []
    for block_index, block_start in enumerate(range(0, group_rows, block_rows)):
        block_queries = queries[block_start : block_start + block_rows]
        block_grad = attended_grad[block_start : block_start + block_rows]
        scores = block_scores(
            block_queries, keys_rot, segment, block_start, block_rows, score_scale
        )
        probability = jnp.exp(scores - log_totals[block_index])
        prob_grad = jnp.einsum(
            "bhe,khe->hbk", block_grad, values_in, preferred_element_type=jnp.float32
        )
        centre = jnp.sum(probability * prob_grad, axis=-1, keepdims=True)
        score_grad = (probability * (prob_grad - centre)).astype(jnp.bfloat16)
        query_parts.append(
            jnp.einsum("hbk,khe->bhe", score_grad, keys_rot, preferred_element_type=jnp.float32)
            * score_scale
        )
        keys_grad = (
            keys_grad
            + jnp.einsum(
                "hbk,bhe->khe", score_grad, block_queries, preferred_element_type=jnp.float32
            )
            * score_scale
        )
        values_grad = values_grad + jnp.einsum(
            "hbk,bhe->khe",
            probability.astype(jnp.bfloat16),
            block_grad,
            preferred_element_type=jnp.float32,
        )
    return (jnp.concatenate(query_parts, axis=0), keys_grad, values_grad)


def fetch_weights(qkv_weight, dense_weight, fc_in_weight, fc_out_weight, layer_index):
    return (
        lax.all_gather(qkv_weight[layer_index], "dp", axis=0, tiled=True),
        lax.all_gather(dense_weight[layer_index], "dp", axis=1, tiled=True),
        lax.all_gather(fc_in_weight[layer_index], "dp", axis=0, tiled=True),
        lax.all_gather(fc_out_weight[layer_index], "dp", axis=1, tiled=True),
    )


def refetch_weights(qkv_weight, dense_weight, fc_in_weight, fc_out_weight, layer_index):
    return (
        lax.all_gather(qkv_weight[layer_index], "dp", axis=0, tiled=True),
        lax.all_gather(dense_weight[layer_index], "dp", axis=1, tiled=True),
        lax.all_gather(fc_in_weight[layer_index], "dp", axis=0, tiled=True),
        lax.all_gather(fc_out_weight[layer_index], "dp", axis=1, tiled=True),
    )


def contract_rows(first_arr, second_arr):
    return lax.dot_general(
        first_arr, second_arr, (((0,), (0,)), ((), ())), preferred_element_type=jnp.float32
    )


def contract_cols(first_arr, second_arr):
    return lax.dot_general(
        first_arr, second_arr, (((1,), (1,)), ((), ())), preferred_element_type=jnp.float32
    )


def local(
    tokens,
    lengths,
    qkv_weight,
    qkv_bias,
    dense_weight,
    dense_bias,
    fc_in_weight,
    fc_in_bias,
    fc_out_weight,
    fc_out_bias,
    norm_gain,
    norm_bias,
    cotangent,
):
    shard_rows = tokens.shape[0]
    layers = qkv_weight.shape[0]
    group_rows = shard_rows * lax.axis_size("tensor")
    block_rows = min(512, group_rows)
    score_scale = HEAD_DIM ** (-0.5)
    segment, position = positions(lengths[0], group_rows)
    half_rot = ROT // 2
    frequency = 10000.0 ** (-(2.0 * jnp.arange(half_rot, dtype=jnp.float32)) / ROT)
    angles = position.astype(jnp.float32)[:, None] * frequency[None, :]
    cosine = jnp.cos(angles)[:, None, :]
    sine_table = jnp.sin(angles)[:, None, :]
    gains_all = norm_gain.astype(jnp.float32)
    shifts_all = norm_bias.astype(jnp.float32)
    stream = tokens.astype(jnp.float32)
    stored_layers = []
    for layer_index in range(layers):
        normed_attn = layer_norm(
            stream, gains_all[layer_index, 0], shifts_all[layer_index, 0]
        ).astype(jnp.bfloat16)
        normed_mlp = layer_norm(
            stream, gains_all[layer_index, 1], shifts_all[layer_index, 1]
        ).astype(jnp.bfloat16)
        group_attn, group_mlp = (
            lax.all_gather(normed_attn, "tensor", axis=0, tiled=True),
            lax.all_gather(normed_mlp, "tensor", axis=0, tiled=True),
        )
        layer_weights = fetch_weights(
            qkv_weight, dense_weight, fc_in_weight, fc_out_weight, layer_index
        )
        w_qkv, w_dense, w_in, w_out = layer_weights
        mixed_proj = jnp.einsum(
            "gd,dcf->gcf", group_attn, w_qkv, preferred_element_type=jnp.float32
        ) + qkv_bias[layer_index].astype(jnp.float32)
        heads_here = mixed_proj.shape[-1] // HEAD_DIM
        head_shape = (group_rows, heads_here, HEAD_DIM)
        queries = rotate(mixed_proj[:, 0].reshape(head_shape), cosine, sine_table).astype(
            jnp.bfloat16
        )
        keys_rot = rotate(mixed_proj[:, 1].reshape(head_shape), cosine, sine_table).astype(
            jnp.bfloat16
        )
        values_in = mixed_proj[:, 2].reshape(head_shape).astype(jnp.bfloat16)
        attended, log_totals = attend(
            queries, keys_rot, values_in, segment, block_rows, score_scale
        )
        attended = attended.reshape(group_rows, heads_here * HEAD_DIM).astype(jnp.bfloat16)
        pre_gelu = jnp.dot(group_mlp, w_in, preferred_element_type=jnp.float32) + fc_in_bias[
            layer_index
        ].astype(jnp.float32)
        hidden = jax.nn.gelu(pre_gelu, approximate=False).astype(jnp.bfloat16)

        def branch_terms(
            start, count, attended=attended, hidden=hidden, w_dense=w_dense, w_out=w_out
        ):
            return jnp.dot(attended, w_dense, preferred_element_type=jnp.float32) + jnp.dot(
                hidden, w_out, preferred_element_type=jnp.float32
            )

        branch = lax.psum_scatter(
            branch_terms(jnp.int32(0), lax.axis_size("tensor") * shard_rows).astype(jnp.bfloat16),
            "tensor",
            scatter_dimension=0,
            tiled=True,
        ).astype(jnp.float32)
        stored_layers.append(
            (
                stream,
                group_attn,
                group_mlp,
                queries,
                keys_rot,
                values_in,
                log_totals,
                attended,
                pre_gelu,
                hidden,
                layer_weights,
            )
        )
        stream = (
            stream
            + branch
            + dense_bias[layer_index].astype(jnp.float32)
            + fc_out_bias[layer_index].astype(jnp.float32)
        )
    output = stream.astype(jnp.bfloat16)
    stream_grad = cotangent.astype(jnp.float32)
    weight_grads = [None] * layers
    column_grads = [None] * layers
    shared_grads = [None] * layers
    for layer_index in reversed(range(layers)):
        (
            stream_in,
            group_attn,
            group_mlp,
            queries,
            keys_rot,
            values_in,
            log_totals,
            attended,
            pre_gelu,
            hidden,
            kept_weights,
        ) = stored_layers[layer_index]
        w_qkv, w_dense, w_in, w_out = refetch_weights(
            qkv_weight, dense_weight, fc_in_weight, fc_out_weight, layer_index
        )
        head_shape = queries.shape
        out_bias_grad = jnp.sum(stream_grad, axis=0)
        grad_rows = lax.all_gather(stream_grad.astype(jnp.bfloat16), "tensor", axis=0, tiled=True)
        dense_grad = contract_rows(attended, grad_rows)
        out_grad = contract_rows(hidden, grad_rows)
        attended_grad = contract_cols(grad_rows, w_dense).astype(jnp.bfloat16).reshape(head_shape)
        hidden_grad = contract_cols(grad_rows, w_out)
        gelu_value, gelu_back = jax.vjp(partial(jax.nn.gelu, approximate=False), pre_gelu)
        pre_grad = gelu_back(hidden_grad)[0].astype(jnp.bfloat16)
        query_grad, keys_grad, values_grad = attend_back(
            queries,
            keys_rot,
            values_in,
            log_totals,
            attended_grad,
            segment,
            block_rows,
            score_scale,
        )
        flat_cols = head_shape[1] * head_shape[2]
        proj_grad = jnp.stack(
            [
                rotate(query_grad, cosine, -sine_table).reshape(group_rows, flat_cols),
                rotate(keys_grad, cosine, -sine_table).reshape(group_rows, flat_cols),
                values_grad.reshape(group_rows, flat_cols),
            ],
            axis=1,
        ).astype(jnp.bfloat16)
        qkv_grad = jnp.einsum(
            "gd,gcf->dcf", group_attn, proj_grad, preferred_element_type=jnp.float32
        )
        qkv_bias_part = jnp.sum(proj_grad.astype(jnp.float32), axis=0)
        in_grad = contract_rows(group_mlp, pre_grad)
        in_bias_part = jnp.sum(pre_grad.astype(jnp.float32), axis=0)
        attn_input_grad = jnp.einsum(
            "gcf,dcf->gd", proj_grad, w_qkv, preferred_element_type=jnp.float32
        )
        mlp_input_grad = contract_cols(pre_grad, w_in)
        attn_share, mlp_share = (
            lax.psum_scatter(
                attn_input_grad.astype(jnp.bfloat16), "tensor", scatter_dimension=0, tiled=True
            ).astype(jnp.float32),
            lax.psum_scatter(
                mlp_input_grad.astype(jnp.bfloat16), "tensor", scatter_dimension=0, tiled=True
            ).astype(jnp.float32),
        )
        normed_one, norm_back_one = jax.vjp(
            layer_norm, stream_in, gains_all[layer_index, 0], shifts_all[layer_index, 0]
        )
        stream_part_one, gain_part_one, shift_part_one = norm_back_one(attn_share)
        normed_two, norm_back_two = jax.vjp(
            layer_norm, stream_in, gains_all[layer_index, 1], shifts_all[layer_index, 1]
        )
        stream_part_two, gain_part_two, shift_part_two = norm_back_two(mlp_share)
        stream_grad = stream_grad + stream_part_one + stream_part_two
        column_grads[layer_index] = (qkv_bias_part, in_bias_part)
        shared_grads[layer_index] = (
            jnp.stack([gain_part_one, gain_part_two]),
            jnp.stack([shift_part_one, shift_part_two]),
            out_bias_grad,
        )
        weight_grads[layer_index] = (
            lax.psum_scatter(
                qkv_grad.astype(jnp.bfloat16), "dp", scatter_dimension=0, tiled=True
            ).astype(jnp.float32),
            lax.psum_scatter(
                dense_grad.astype(jnp.bfloat16), "dp", scatter_dimension=1, tiled=True
            ).astype(jnp.float32),
            lax.psum_scatter(
                in_grad.astype(jnp.bfloat16), "dp", scatter_dimension=0, tiled=True
            ).astype(jnp.float32),
            lax.psum_scatter(
                out_grad.astype(jnp.bfloat16), "dp", scatter_dimension=1, tiled=True
            ).astype(jnp.float32),
        )
    stacked = tuple(
        (
            jnp.stack([weight_grads[layer_index][member] for layer_index in range(layers)])
            for member in range(4)
        )
    )
    qkv_bias_grad, fc_in_bias_grad = lax.psum(
        (
            jnp.stack([column_grads[layer_index][0] for layer_index in range(layers)]),
            jnp.stack([column_grads[layer_index][1] for layer_index in range(layers)]),
        ),
        "dp",
    )
    norm_gain_grad, norm_bias_grad, bias_grad = lax.psum(
        (
            jnp.stack([shared_grads[layer_index][0] for layer_index in range(layers)]),
            jnp.stack([shared_grads[layer_index][1] for layer_index in range(layers)]),
            jnp.stack([shared_grads[layer_index][2] for layer_index in range(layers)]),
        ),
        ("dp", "tensor"),
    )
    return (
        output,
        stream_grad,
        stacked[0],
        qkv_bias_grad,
        stacked[1],
        bias_grad,
        stacked[2],
        fc_in_bias_grad,
        stacked[3],
        bias_grad,
        norm_gain_grad,
        norm_bias_grad,
    )


def solution(mesh):
    return jax.shard_map(
        local,
        mesh=mesh,
        in_specs=(
            P(("dp", "tensor"), None),
            P("dp", None),
            P(None, "dp", None, "tensor"),
            P(None, None, "tensor"),
            P(None, "tensor", "dp"),
            P(),
            P(None, "dp", "tensor"),
            P(None, "tensor"),
            P(None, "tensor", "dp"),
            P(),
            P(),
            P(),
            P(("dp", "tensor"), None),
        ),
        out_specs=(
            P(("dp", "tensor"), None),
            P(("dp", "tensor"), None),
            P(None, "dp", None, "tensor"),
            P(None, None, "tensor"),
            P(None, "tensor", "dp"),
            P(),
            P(None, "dp", "tensor"),
            P(None, "tensor"),
            P(None, "tensor", "dp"),
            P(),
            P(),
            P(),
        ),
        check_vma=False,
    )
```

profile of v0, /device:TPU:1, one launch (start us, length us, event | category | flops | bytes accessed | tf_op | source)
XLA Modules:
  0.0 1523.4 jit_solution(10226132703851349249)
XLA Ops:
  16.4 24.4 %all-gather = bf16[1,1024,3,128]{3,1,2,0:T(8,128)(2,1)S(1)} all-gather(bf16[1,64,3,128]{3,1,2,0:T(8,128)(2,1)S(1)} %get-tuple-element.120), channel_id=2, replica_groups=mesh['dp'=16,'tensor'=8] {'dp'}, dimensions={1}, use_global_device_ids=true | all-gather | bytes 835584 | tf_op jit(solution)/shard_map/all_gather | solution.py:126
  84.4 20.2 %all-gather.31.cloned.1.call-done = bf16[1,1024,512]{2,1,0:T(8,128)(2,1)} async-done(((bf16[1,64,512]{2,1,0:T(8,128)(2,1)}), bf16[1,1024,512]{2,1,0:T(8,128)(2,1)}) %all-gather.31.cloned.1.call-update) | async-done | bytes 1048592 | tf_op jit(solution)/shard_map/all_gather | solution.py:128
  104.6 56.0 %all-gather.21.cloned.1.call-done = bf16[1024,1024]{1,0:T(8,128)(2,1)} async-done(((bf16[128,1024]{1,0:T(8,128)(2,1)}), bf16[1024,1024]{1,0:T(8,128)(2,1)}) %all-gather.21.cloned.1.call-update) | async-done | bytes 2097168 | tf_op jit(solution)/shard_map/all_gather | solution.py:193
  169.1 24.4 %all-gather.33.cloned.1.call-done = bf16[1,512,1024]{1,2,0:T(8,128)(2,1)} async-done(((bf16[1,512,64]{1,2,0:T(8,128)(2,1)}), bf16[1,512,1024]{1,2,0:T(8,128)(2,1)}) %all-gather.33.cloned.1.call-update) | async-done | bytes 1048592 | tf_op jit(solution)/shard_map/all_gather | solution.py:129
  200.4 71.4 %reduce-scatter.15.cloned.1.call-done = bf16[128,1024]{1,0:T(8,128)(2,1)} async-done(((bf16[1024,1024]{1,0:T(8,128)(2,1)}), bf16[128,1024]{1,0:T(8,128)(2,1)}) %reduce-scatter.15.cloned.1.call-update) | async-done | bytes 262160 | tf_op jit(solution)/shard_map/reduce_scatter | solution.py:227
  278.3 24.2 %all-gather.4 = bf16[1,1024,3,128]{3,1,2,0:T(8,128)(2,1)S(1)} all-gather(bf16[1,64,3,128]{3,1,2,0:T(8,128)(2,1)S(1)} %get-tuple-element.119), channel_id=6, replica_groups=mesh['dp'=16,'tensor'=8] {'dp'}, dimensions={1}, use_global_device_ids=true | all-gather | bytes 835584 | tf_op jit(solution)/shard_map/all_gather | solution.py:126
  331.5 52.2 %all-gather.23.cloned.1.call-done = bf16[1024,1024]{1,0:T(8,128)(2,1)} async-done(((bf16[128,1024]{1,0:T(8,128)(2,1)}), bf16[1024,1024]{1,0:T(8,128)(2,1)}) %all-gather.23.cloned.1.call-update) | async-done | bytes 2097168 | tf_op jit(solution)/shard_map/all_gather | solution.py:192
  426.2 47.0 %all-gather.25.cloned.1.call-done = bf16[1024,1024]{1,0:T(8,128)(2,1)} async-done(((bf16[128,1024]{1,0:T(8,128)(2,1)}), bf16[1024,1024]{1,0:T(8,128)(2,1)}) %all-gather.25.cloned.1.call-update) | async-done | bytes 2097168 | tf_op jit(solution)/shard_map/all_gather | solution.py:193
  482.0 24.1 %all-gather.37.cloned.1.call-done = bf16[1,512,1024]{1,2,0:T(8,128)(2,1)} async-done(((bf16[1,512,64]{1,2,0:T(8,128)(2,1)}), bf16[1,512,1024]{1,2,0:T(8,128)(2,1)}) %all-gather.37.cloned.1.call-update) | async-done | bytes 1048592 | tf_op jit(solution)/shard_map/all_gather | solution.py:129
  524.6 58.4 %reduce-scatter.19.cloned.1.call-done = bf16[128,1024]{1,0:T(8,128)(2,1)} async-done(((bf16[1024,1024]{1,0:T(8,128)(2,1)}), bf16[128,1024]{1,0:T(8,128)(2,1)}) %reduce-scatter.19.cloned.1.call-update) | async-done | bytes 262160 | tf_op jit(solution)/shard_map/reduce_scatter | solution.py:315
  583.0 77.4 %reduce-scatter.21.cloned.1.call-done = bf16[128,1024]{1,0:T(8,128)(2,1)} async-done(((bf16[1024,1024]{1,0:T(8,128)(2,1)}), bf16[128,1024]{1,0:T(8,128)(2,1)}) %reduce-scatter.21.cloned.1.call-update) | async-done | bytes 262160 | tf_op jit(solution)/shard_map/reduce_scatter | solution.py:318
  665.7 72.2 %reduce-scatter.17.cloned.1.call-done = bf16[128,1024]{1,0:T(8,128)(2,1)} async-done(((bf16[1024,1024]{1,0:T(8,128)(2,1)}), bf16[128,1024]{1,0:T(8,128)(2,1)}) %reduce-scatter.17.cloned.1.call-update) | async-done | bytes 262160 | tf_op jit(solution)/shard_map/reduce_scatter | solution.py:227
  744.4 51.1 %all-gather.29.cloned.1.call-done = bf16[1024,1024]{1,0:T(8,128)(2,1)} async-done(((bf16[128,1024]{1,0:T(8,128)(2,1)}), bf16[1024,1024]{1,0:T(8,128)(2,1)}) %all-gather.29.cloned.1.call-update) | async-done | bytes 2097168 | tf_op jit(solution)/shard_map/all_gather | solution.py:278
  857.2 28.5 %all-reduce.1 = (f32[2,3,128]{2,1,0:T(4,128)S(1)}, f32[2,512]{1,0:T(2,128)}) all-reduce(f32[2,3,128]{2,1,0:T(4,128)S(1)} %pad_maximum_fusion.17, f32[2,512]{1,0:T(2,128)S(1)} %pad_maximum_fusion.18), channel_id=1, replica_groups=mesh['dp'=16,'tensor'=8] {'dp'}, use_global_device_ids=true, to_apply=%region_37.38 | all-reduce | flops 1792 | bytes 14336 | tf_op jit(solution)/shard_map/psum | solution.py:357
  886.3 27.4 %reduce-scatter.31.cloned.1.call-done = bf16[128,64]{0,1:T(8,128)(2,1)} async-done(((bf16[128,1024]{0,1:T(8,128)(2,1)}), bf16[128,64]{0,1:T(8,128)(2,1)}) %reduce-scatter.31.cloned.1.call-update) | async-done | bytes 16400 | tf_op jit(solution)/shard_map/reduce_scatter | solution.py:341
  915.1 60.5 %reduce-scatter.29.cloned.1.call-done = bf16[64,3,128]{2,0,1:T(8,128)(2,1)} async-done(((bf16[1024,3,128]{2,0,1:T(8,128)(2,1)}), bf16[64,3,128]{2,0,1:T(8,128)(2,1)}) %reduce-scatter.29.cloned.1.call-update) | async-done | bytes 49168 | tf_op jit(solution)/shard_map/reduce_scatter | solution.py:338
  975.6 62.1 %reduce-scatter.27.cloned.1.call-done = bf16[64,3,128]{2,0,1:T(8,128)(2,1)} async-done(((bf16[1024,3,128]{2,0,1:T(8,128)(2,1)}), bf16[64,3,128]{2,0,1:T(8,128)(2,1)}) %reduce-scatter.27.cloned.1.call-update) | async-done | bytes 49168 | tf_op jit(solution)/shard_map/reduce_scatter | solution.py:338
  1039.2 61.1 %reduce-scatter.37.cloned.1.call-done = bf16[64,512]{1,0:T(8,128)(2,1)} async-done(((bf16[1024,512]{1,0:T(8,128)(2,1)}), bf16[64,512]{1,0:T(8,128)(2,1)}) %reduce-scatter.37.cloned.1.call-update) | async-done | bytes 65552 | tf_op jit(solution)/shard_map/reduce_scatter | solution.py:344
  1100.3 62.2 %reduce-scatter.35.cloned.1.call-done = bf16[64,512]{1,0:T(8,128)(2,1)} async-done(((bf16[1024,512]{1,0:T(8,128)(2,1)}), bf16[64,512]{1,0:T(8,128)(2,1)}) %reduce-scatter.35.cloned.1.call-update) | async-done | bytes 65552 | tf_op jit(solution)/shard_map/reduce_scatter | solution.py:344
  1164.2 60.7 %reduce-scatter.41.cloned.1.call-done = bf16[512,64]{0,1:T(8,128)(2,1)} async-done(((bf16[512,1024]{0,1:T(8,128)(2,1)}), bf16[512,64]{0,1:T(8,128)(2,1)}) %reduce-scatter.41.cloned.1.call-update) | async-done | bytes 65552 | tf_op jit(solution)/shard_map/reduce_scatter | solution.py:347
  1224.9 62.4 %reduce-scatter.39.cloned.1.call-done = bf16[512,64]{0,1:T(8,128)(2,1)} async-done(((bf16[512,1024]{0,1:T(8,128)(2,1)}), bf16[512,64]{0,1:T(8,128)(2,1)}) %reduce-scatter.39.cloned.1.call-update) | async-done | bytes 65552 | tf_op jit(solution)/shard_map/reduce_scatter | solution.py:347
  1288.9 77.6 %reduce-scatter.23.cloned.1.call-done = bf16[128,1024]{1,0:T(8,128)(2,1)} async-done(((bf16[1024,1024]{1,0:T(8,128)(2,1)}), bf16[128,1024]{1,0:T(8,128)(2,1)}) %reduce-scatter.23.cloned.1.call-update) | async-done | bytes 262160 | tf_op jit(solution)/shard_map/reduce_scatter | solution.py:315
  1366.6 77.3 %reduce-scatter.25.cloned.1.call-done = bf16[128,1024]{1,0:T(8,128)(2,1)} async-done(((bf16[1024,1024]{1,0:T(8,128)(2,1)}), bf16[128,1024]{1,0:T(8,128)(2,1)}) %reduce-scatter.25.cloned.1.call-update) | async-done | bytes 262160 | tf_op jit(solution)/shard_map/reduce_scatter | solution.py:318
  1447.0 66.3 %all-reduce = (f32[2,1024]{1,0:T(2,128)S(1)}, f32[2,2,1024]{2,1,0:T(2,128)}, f32[2,2,1024]{2,1,0:T(2,128)}) all-reduce(f32[2,1024]{1,0:T(2,128)S(1)} %pad_maximum_fusion.16, f32[2,2,1024]{2,1,0:T(2,128)S(1)} %pad_maximum_fusion.14, f32[2,2,1024]{2,1,0:T(2,128)S(1)} %pad_maximum_fusion.15), channel_id=1, replica_groups=mesh['dp'=16,'tensor'=8] {'dp','tensor'}, use_global_device_ids=true, to_apply=%region_42.43 | all-reduce | flops 10240 | bytes 81920 | tf_op jit(solution)/shard_map/psum | solution.py:364
  (428 shorter events, 257.7 us)
Async XLA Ops:
  7.2 63.8 %all-gather.19.cloned.1.call-start = ((), (), s32[]{:S(2)}) async-start(), calls=%async_computation.14 | async-start | bytes 2359296 | tf_op jit(solution)/shard_map/all_gather | solution.py:192
  13.2 91.4 %all-gather.31.cloned.1.call-start = ((), (), s32[]{:S(2)}) async-start(), calls=%async_computation.34 | async-start | bytes 1114112 | tf_op jit(solution)/shard_map/all_gather | solution.py:128
  14.8 145.8 %all-gather.21.cloned.1.call-start = ((), (), s32[]{:S(2)}) async-start(), calls=%async_computation.15 | async-start | bytes 2359296 | tf_op jit(solution)/shard_map/all_gather | solution.py:193
  15.5 177.9 %all-gather.33.cloned.1.call-start = ((), (), s32[]{:S(2)}) async-start(), calls=%async_computation.35 | async-start | bytes 1114112 | tf_op jit(solution)/shard_map/all_gather | solution.py:129
  16.3 255.5 %reduce-scatter.15.cloned.1.call-start = ((), (), s32[]{:S(2)}) async-start(), calls=%async_computation.16 | async-start | bytes 2359296 | tf_op jit(solution)/shard_map/reduce_scatter | solution.py:227
  198.6 130.4 %all-gather.27.cloned.1.call-start = ((), (), s32[]{:S(2)}) async-start(), calls=%async_computation.20 | async-start | bytes 2359296 | tf_op jit(solution)/shard_map/all_gather | solution.py:278
  199.2 184.5 %all-gather.23.cloned.1.call-start = ((), (), s32[]{:S(2)}) async-start(), calls=%async_computation.17 | async-start | bytes 2359296 | tf_op jit(solution)/shard_map/all_gather | solution.py:192
  276.2 150.1 %all-gather.35.cloned.1.call-start = ((), (), s32[]{:S(2)}) async-start(), calls=%async_computation.36 | async-start | bytes 1114112 | tf_op jit(solution)/shard_map/all_gather | solution.py:128
  276.9 196.3 %all-gather.25.cloned.1.call-start = ((), (), s32[]{:S(2)}) async-start(), calls=%async_computation.18 | async-start | bytes 2359296 | tf_op jit(solution)/shard_map/all_gather | solution.py:193
  277.7 228.5 %all-gather.37.cloned.1.call-start = ((), (), s32[]{:S(2)}) async-start(), calls=%async_computation.37 | async-start | bytes 1114112 | tf_op jit(solution)/shard_map/all_gather | solution.py:129
  278.2 304.8 %reduce-scatter.19.cloned.1.call-start = ((), (), s32[]{:S(2)}) async-start(), calls=%async_computation.21 | async-start | bytes 2359296 | tf_op jit(solution)/shard_map/reduce_scatter | solution.py:315
  426.2 234.2 %reduce-scatter.21.cloned.1.call-start = ((), (), s32[]{:S(2)}) async-start(), calls=%async_computation.22 | async-start | bytes 2359296 | tf_op jit(solution)/shard_map/reduce_scatter | solution.py:318
  515.0 222.9 %reduce-scatter.17.cloned.1.call-start = ((), (), s32[]{:S(2)}) async-start(), calls=%async_computation.19 | async-start | bytes 2359296 | tf_op jit(solution)/shard_map/reduce_scatter | solution.py:227
  524.6 271.0 %all-gather.29.cloned.1.call-start = ((), (), s32[]{:S(2)}) async-start(), calls=%async_computation.23 | async-start | bytes 2359296 | tf_op jit(solution)/shard_map/all_gather | solution.py:278
  741.7 144.7 %reduce-scatter.33.cloned.1.call-start = ((), (), s32[]{:S(2)}) async-start(), calls=%async_computation.29 | async-start | bytes 278528 | tf_op jit(solution)/shard_map/reduce_scatter | solution.py:341
  744.3 169.4 %reduce-scatter.31.cloned.1.call-start = ((), (), s32[]{:S(2)}) async-start(), calls=%async_computation.28 | async-start | bytes 278528 | tf_op jit(solution)/shard_map/reduce_scatter | solution.py:341
  798.8 176.8 %reduce-scatter.29.cloned.1.call-start = ((), (), s32[]{:S(2)}) async-start(), calls=%async_computation.27 | async-start | bytes 835584 | tf_op jit(solution)/shard_map/reduce_scatter | solution.py:338
  802.9 234.7 %reduce-scatter.27.cloned.1.call-start = ((), (), s32[]{:S(2)}) async-start(), calls=%async_computation.26 | async-start | bytes 835584 | tf_op jit(solution)/shard_map/reduce_scatter | solution.py:338
  828.0 272.3 %reduce-scatter.37.cloned.1.call-start = ((), (), s32[]{:S(2)}) async-start(), calls=%async_computation.31 | async-start | bytes 1114112 | tf_op jit(solution)/shard_map/reduce_scatter | solution.py:344
  832.3 330.2 %reduce-scatter.35.cloned.1.call-start = ((), (), s32[]{:S(2)}) async-start(), calls=%async_computation.30 | async-start | bytes 1114112 | tf_op jit(solution)/shard_map/reduce_scatter | solution.py:344
  840.4 384.5 %reduce-scatter.41.cloned.1.call-start = ((), (), s32[]{:S(2)}) async-start(), calls=%async_computation.33 | async-start | bytes 1114112 | tf_op jit(solution)/shard_map/reduce_scatter | solution.py:347
  844.3 443.0 %reduce-scatter.39.cloned.1.call-start = ((), (), s32[]{:S(2)}) async-start(), calls=%async_computation.32 | async-start | bytes 1114112 | tf_op jit(solution)/shard_map/reduce_scatter | solution.py:347
  848.7 517.9 %reduce-scatter.23.cloned.1.call-start = ((), (), s32[]{:S(2)}) async-start(), calls=%async_computation.24 | async-start | bytes 2359296 | tf_op jit(solution)/shard_map/reduce_scatter | solution.py:315
  851.4 592.5 %reduce-scatter.25.cloned.1.call-start = ((), (), s32[]{:S(2)}) async-start(), calls=%async_computation.25 | async-start | bytes 2359296 | tf_op jit(solution)/shard_map/reduce_scatter | solution.py:318
  (108 other events, 5025.2 us)
Sparse Core Ops, SparseCore 0:
  13.3 57.7 all-gather.18
  73.3 31.2 all-gather.30
  107.5 53.0 all-gather.20
  162.1 31.2 all-gather.32
  198.7 73.0 reduce-scatter.14
  274.0 54.9 all-gather.26
  332.0 51.6 all-gather.22
  385.9 31.2 all-gather.34
  420.2 53.0 all-gather.24
  474.8 31.2 all-gather.36
  509.8 73.1 reduce-scatter.18
  586.6 73.7 reduce-scatter.20
  664.1 73.7 reduce-scatter.16
  741.8 53.7 all-gather.28
  797.7 54.9 reduce-scatter.32
  855.1 58.6 reduce-scatter.30
  916.0 59.6 reduce-scatter.28
  978.0 59.6 reduce-scatter.26
  1040.1 60.2 reduce-scatter.36
  1102.7 59.8 reduce-scatter.34
  1165.0 59.9 reduce-scatter.40
  1227.4 59.8 reduce-scatter.38
  1291.1 75.4 reduce-scatter.22
  1370.2 73.7 reduce-scatter.24
where the time goes:
time: 1540 us; the launch traced here: 1520 us
  waiting for transfers between devices  1130 us (73%)
  blocking collectives  179 us (12%)
  matrix products  133 us (9%)
  other arithmetic  46.4 us (3%)
  local copies, waits for them, and re-layouts  21.8 us (1%)
  between operations  16.5 us (1%)
    reduce_scatter x2, waiting for transfers between devices, local(): lax.psum_scatter(mlp_input_grad.astype(jnp.bfloat16), 'tensor', scatter_d...  155 us
    reduce_scatter x2, waiting for transfers between devices, local(): lax.psum_scatter(branch_terms(jnp.int32(0), lax.axis_size('tensor') * sha...  144 us
    reduce_scatter x2, waiting for transfers between devices, local(): lax.psum_scatter(attn_input_grad.astype(jnp.bfloat16), 'tensor', scatter_...  136 us
    reduce_scatter x2, waiting for transfers between devices, local(): lax.psum_scatter(in_grad.astype(jnp.bfloat16), 'dp', scatter_dimension=0,...  123 us
    reduce_scatter x2, waiting for transfers between devices, local(): lax.psum_scatter(out_grad.astype(jnp.bfloat16), 'dp', scatter_dimension=1...  123 us
    reduce_scatter x2, waiting for transfers between devices, local(): lax.psum_scatter(qkv_grad.astype(jnp.bfloat16), 'dp', scatter_dimension=0...  123 us
    all_gather x2, waiting for transfers between devices, local(): lax.all_gather(normed_mlp, 'tensor', axis=0, tiled=True)  103 us
    psum x1, blocking collectives, local(): lax.psum((jnp.stack([shared_grads[layer_index][0] for layer_index in rang...  66.3 us
  transfers between devices with their start and end apart: 24, of which 22 were waited for; matrix products, arithmetic and copies ran while one was open for 11% of the time, Pallas kernels for 0%

commit v1 on v0

v1 whole, which is shorter than its diff:
```python
from functools import partial

import jax
import jax.numpy as jnp
from jax import lax
from jax.experimental import pallas as pl
from jax.experimental.pallas import tpu as pltpu
from jax.sharding import PartitionSpec as P

MESH = pl.DeviceIdType.MESH
HEAD_DIM = 64
ROT = 16
EPSILON = 1e-05
MASKED = -1000000000.0
BF = jnp.bfloat16
F32 = jnp.float32
ANY = pl.BlockSpec(memory_space=pl.ANY)
VM = pl.BlockSpec(memory_space=pltpu.VMEM)

T_DELTAS = [(y, h) for y in (1, 3, 2, 0) for h in (0, 1) if y or h]
C_DELTAS = [(a, z) for z in (1, 3, 2, 0) for a in (0, 1) if a or z]


def coords():
    d = lax.axis_index("dp")
    t = lax.axis_index("tensor")
    return d // 8, lax.rem(d // 2, 4), lax.rem(d, 2), t // 2, lax.rem(t, 2)


def t_peer(y, h, delta):
    return lax.rem(y + delta[0], 4) * 2 + lax.rem(h + delta[1], 2)


def c_peer(a, z, delta):
    return lax.rem(a + delta[0], 2) * 4 + lax.rem(z + delta[1], 4)


def greet(d, t, tensor_peers, dp_peers):
    barrier = pltpu.get_barrier_semaphore()
    for p in tensor_peers:
        pl.semaphore_signal(barrier, inc=1, device_id=(d, p), device_id_type=MESH)
    for p in dp_peers:
        pl.semaphore_signal(barrier, inc=1, device_id=(p, t), device_id_type=MESH)
    pl.semaphore_wait(barrier, len(tensor_peers) + len(dp_peers))


def send(src, dst, ssem, rsem, device):
    copy = pltpu.make_async_remote_copy(
        src_ref=src, dst_ref=dst, send_sem=ssem, recv_sem=rsem, device_id=device, device_id_type=MESH
    )
    copy.start()
    return copy


def tensor_gather_start(src, dst, d, t, tp, ssem, rsem):
    rows = src.shape[0]
    place = dst.at[pl.ds(pl.multiple_of(t * rows, rows), rows)]
    return [send(src, place, ssem.at[i], rsem.at[i], (d, p)) for i, p in enumerate(tp)]


def tensor_scatter_start(src, buf, d, tp, ssem, rsem):
    rows = buf.shape[1]
    return [
        send(src.at[pl.ds(pl.multiple_of(p * rows, rows), rows)], buf.at[i], ssem.at[i], rsem.at[i], (d, p))
        for i, p in enumerate(tp)
    ]


def dp_gather_start(src, dst, chip, core, t, cp, ssem, rsem):
    rows = src.shape[0]
    place = dst.at[pl.ds(pl.multiple_of((chip * 2 + core) * rows, rows), rows)]
    first = [send(src, place, ssem.at[i], rsem.at[i], (p * 2 + core, t)) for i, p in enumerate(cp)]
    mine = send(src, place, ssem.at[7], rsem.at[7], (chip * 2 + 1 - core, t))
    return first, mine


def dp_gather_finish(first, mine, dst, rows, chip, core, t, sources, ssem, rsem):
    second = []
    for i, s in enumerate(sources):
        first[i].wait_recv()
        place = dst.at[pl.ds(pl.multiple_of((s * 2 + core) * rows, rows), rows)]
        second.append(send(place, place, ssem.at[8 + i], rsem.at[8 + i], (chip * 2 + 1 - core, t)))
    for c in first:
        c.wait_send()
    mine.wait()
    for c in second:
        c.wait()


def peers():
    a, z, core, y, h = coords()
    d = lax.axis_index("dp")
    t = lax.axis_index("tensor")
    chip = a * 4 + z
    tp = [t_peer(y, h, x) for x in T_DELTAS]
    cp = [c_peer(a, z, x) for x in C_DELTAS]
    back = [c_peer(a, z, (x[0], (4 - x[1]) % 4)) for x in C_DELTAS]
    return d, t, chip, core, tp, cp, back


def open_kernel(x_ref, w_ref, xg_ref, wg_ref, ts, tr, ds_, dr, ls):
    d, t, chip, core, tp, cp, back = peers()
    rows = x_ref.shape[0]
    wrows = w_ref.shape[0]
    own = pltpu.make_async_copy(x_ref, xg_ref.at[pl.ds(pl.multiple_of(t * rows, rows), rows)], ls.at[0])
    own.start()
    own_w = pltpu.make_async_copy(w_ref, wg_ref.at[pl.ds(pl.multiple_of(d * wrows, wrows), wrows)], ls.at[1])
    own_w.start()
    greet(d, t, tp, [p * 2 + core for p in cp] + [chip * 2 + 1 - core])
    xs = tensor_gather_start(x_ref, xg_ref, d, t, tp, ts, tr)
    first, mine = dp_gather_start(w_ref, wg_ref, chip, core, t, cp, ds_, dr)
    dp_gather_finish(first, mine, wg_ref, wrows, chip, core, t, back, ds_, dr)
    for c in xs:
        c.wait()
    own.wait()
    own_w.wait()


def open_call(x, w, cid):
    return pl.pallas_call(
        open_kernel,
        out_shape=(
            jax.ShapeDtypeStruct((x.shape[0] * 8, x.shape[1]), x.dtype),
            jax.ShapeDtypeStruct((w.shape[0] * 16, w.shape[1]), w.dtype),
        ),
        in_specs=[ANY, ANY],
        out_specs=(ANY, ANY),
        scratch_shapes=[
            pltpu.SemaphoreType.DMA((7,)),
            pltpu.SemaphoreType.DMA((7,)),
            pltpu.SemaphoreType.DMA((15,)),
            pltpu.SemaphoreType.DMA((15,)),
            pltpu.SemaphoreType.DMA((2,)),
        ],
        compiler_params=pltpu.CompilerParams(collective_id=cid, has_side_effects=True),
        cost_estimate=pl.CostEstimate(flops=0, bytes_accessed=80_000_000, transcendentals=0),
        name="gather_weights_and_rows",
    )(x, w)


def summed(own, buf):
    total = own.astype(F32)
    for i in range(7):
        total = total + buf[i].astype(F32)
    return total


def normed(x):
    average = jnp.mean(x, axis=-1, keepdims=True)
    centered = x - average
    inv = lax.rsqrt(jnp.mean(centered * centered, axis=-1, keepdims=True) + EPSILON)
    return centered * inv, inv


def middle_kernel(
    part_ref, stream_ref, bias_ref, w_ref, stream_out, xg_ref, wg_ref,
    own_v, buf, xhat_v, rs_s, rs_r, ts, tr, ds_, dr, ls,
):
    d, t, chip, core, tp, cp, back = peers()
    rows = stream_ref.shape[0]
    wrows = w_ref.shape[0]
    own = pltpu.make_async_copy(part_ref.at[pl.ds(pl.multiple_of(t * rows, rows), rows)], own_v, ls.at[0])
    own.start()
    own_w = pltpu.make_async_copy(w_ref, wg_ref.at[pl.ds(pl.multiple_of(d * wrows, wrows), wrows)], ls.at[1])
    own_w.start()
    greet(d, t, tp, [p * 2 + core for p in cp] + [chip * 2 + 1 - core])
    rs = tensor_scatter_start(part_ref, buf, d, tp, rs_s, rs_r)
    first, mine = dp_gather_start(w_ref, wg_ref, chip, core, t, cp, ds_, dr)
    own.wait()
    for c in rs:
        c.wait()
    stream = stream_ref[...] + summed(own_v[...], buf) + bias_ref[...]
    stream_out[...] = stream
    xhat_v[...] = normed(stream)[0].astype(BF)
    own2 = pltpu.make_async_copy(xhat_v, xg_ref.at[pl.ds(pl.multiple_of(t * rows, rows), rows)], ls.at[0])
    own2.start()
    xs = tensor_gather_start(xhat_v, xg_ref, d, t, tp, ts, tr)
    dp_gather_finish(first, mine, wg_ref, wrows, chip, core, t, back, ds_, dr)
    for c in xs:
        c.wait()
    own2.wait()
    own_w.wait()


def middle_call(part, stream, bias, w, cid):
    rows, width = stream.shape
    dma = pltpu.SemaphoreType.DMA
    return pl.pallas_call(
        middle_kernel,
        out_shape=(
            jax.ShapeDtypeStruct(stream.shape, F32),
            jax.ShapeDtypeStruct(part.shape, BF),
            jax.ShapeDtypeStruct((w.shape[0] * 16, w.shape[1]), w.dtype),
        ),
        in_specs=[ANY, VM, VM, ANY],
        out_specs=(VM, ANY, ANY),
        scratch_shapes=[
            pltpu.VMEM((rows, width), BF),
            pltpu.VMEM((7, rows, width), BF),
            pltpu.VMEM((rows, width), BF),
            dma((7,)), dma((7,)), dma((7,)), dma((7,)), dma((15,)), dma((15,)), dma((2,)),
        ],
        compiler_params=pltpu.CompilerParams(
            collective_id=cid, has_side_effects=True, vmem_limit_bytes=32 * 2**20
        ),
        cost_estimate=pl.CostEstimate(flops=0, bytes_accessed=150_000_000, transcendentals=0),
        name="sum_rows_and_gather",
    )(part, stream, bias, w)


def dp_scatter_core(dw_ref, mine_v, core_buf, chip, core, t, ssem, rsem, lsem):
    mine = pltpu.make_async_copy(dw_ref.at[:, core], mine_v, lsem)
    mine.start()
    swap = send(dw_ref.at[:, 1 - core], core_buf, ssem, rsem, (chip * 2 + 1 - core, t))
    return mine, swap


def dp_scatter_chips(mine, swap, mine_v, core_buf, chip_buf, core, t, cp, ssem, rsem):
    mine.wait()
    swap.wait()
    copies = []
    for i, p in enumerate(cp):
        mine_v[p] = (mine_v[p].astype(F32) + core_buf[p].astype(F32)).astype(BF)
        copies.append(send(mine_v.at[p], chip_buf.at[i], ssem.at[i], rsem.at[i], (p * 2 + core, t)))
    return copies


def dp_scatter_finish(copies, mine_v, core_buf, chip_buf, chip, out_ref):
    for c in copies:
        c.wait()
    total = mine_v[chip].astype(F32) + core_buf[chip].astype(F32)
    for i in range(7):
        total = total + chip_buf[i].astype(F32)
    out_ref[...] = total


def stream_back(total, grad, stream):
    xhat, inv = normed(stream)
    first = jnp.mean(total, axis=-1, keepdims=True)
    second = jnp.mean(total * xhat, axis=-1, keepdims=True)
    return grad + inv * (total - first - xhat * second)


def turn_kernel(
    part_ref, grad_ref, stream_ref, dw_ref, grad_out, gg_ref, dw_out,
    own_v, buf, low_v, mine_v, core_buf, chip_buf, rs_s, rs_r, ts, tr, ds_, dr, ls,
):
    d, t, chip, core, tp, cp, back = peers()
    rows = stream_ref.shape[0]
    own = pltpu.make_async_copy(part_ref.at[pl.ds(pl.multiple_of(t * rows, rows), rows)], own_v, ls.at[0])
    own.start()
    greet(d, t, tp, [p * 2 + core for p in cp] + [chip * 2 + 1 - core])
    mine, swap = dp_scatter_core(dw_ref, mine_v, core_buf, chip, core, t, ds_.at[7], dr.at[7], ls.at[1])
    rs = tensor_scatter_start(part_ref, buf, d, tp, rs_s, rs_r)
    copies = dp_scatter_chips(mine, swap, mine_v, core_buf, chip_buf, core, t, cp, ds_, dr)
    own.wait()
    for c in rs:
        c.wait()
    grad = stream_back(summed(own_v[...], buf), grad_ref[...], stream_ref[...])
    grad_out[...] = grad
    low_v[...] = grad.astype(BF)
    own2 = pltpu.make_async_copy(low_v, gg_ref.at[pl.ds(pl.multiple_of(t * rows, rows), rows)], ls.at[0])
    own2.start()
    xs = tensor_gather_start(low_v, gg_ref, d, t, tp, ts, tr)
    dp_scatter_finish(copies, mine_v, core_buf, chip_buf, chip, dw_out)
    for c in xs:
        c.wait()
    own2.wait()


def turn_call(part, grad, stream, dw, cid):
    rows, width = stream.shape
    wrows, wcols = dw.shape[0] // 16, dw.shape[1]
    dma = pltpu.SemaphoreType.DMA
    return pl.pallas_call(
        turn_kernel,
        out_shape=(
            jax.ShapeDtypeStruct(stream.shape, F32),
            jax.ShapeDtypeStruct(part.shape, BF),
            jax.ShapeDtypeStruct((wrows, wcols), F32),
        ),
        in_specs=[ANY, VM, VM, ANY],
        out_specs=(VM, ANY, VM),
        scratch_shapes=[
            pltpu.VMEM((rows, width), BF),
            pltpu.VMEM((7, rows, width), BF),
            pltpu.VMEM((rows, width), BF),
            pltpu.VMEM((8, wrows, wcols), BF),
            pltpu.VMEM((8, wrows, wcols), BF),
            pltpu.VMEM((7, wrows, wcols), BF),
            dma((7,)), dma((7,)), dma((7,)), dma((7,)), dma((8,)), dma((8,)), dma((2,)),
        ],
        compiler_params=pltpu.CompilerParams(
            collective_id=cid, has_side_effects=True, vmem_limit_bytes=32 * 2**20
        ),
        cost_estimate=pl.CostEstimate(flops=0, bytes_accessed=150_000_000, transcendentals=0),
        name="sum_gradients_and_gather",
    )(part, grad, stream, dw.reshape(8, 2, wrows, wcols))


def last_kernel(
    part_ref, grad_ref, stream_ref, dw_ref, small_ref, cols_ref, grad_out, dw_out, small_out, cols_out,
    own_v, buf, mine_v, core_buf, chip_buf, small_buf, both_v, both_buf, sum_v,
    rs_s, rs_r, ds_, dr, ls, ss, sr, bs, br, gs, gr,
):
    d, t, chip, core, tp, cp, back = peers()
    rows = stream_ref.shape[0]
    own = pltpu.make_async_copy(part_ref.at[pl.ds(pl.multiple_of(t * rows, rows), rows)], own_v, ls.at[0])
    own.start()
    others = [p * 2 + core for p in cp] + [p * 2 + 1 - core for p in cp] + [chip * 2 + 1 - core]
    greet(d, t, tp, others)
    mine, swap = dp_scatter_core(dw_ref, mine_v, core_buf, chip, core, t, ds_.at[7], dr.at[7], ls.at[1])
    small = [
        send(small_ref.at[p], small_buf.at[i], ss.at[i], sr.at[i], (d, p)) for i, p in enumerate(tp)
    ]
    rs = tensor_scatter_start(part_ref, buf, d, tp, rs_s, rs_r)
    copies = dp_scatter_chips(mine, swap, mine_v, core_buf, chip_buf, core, t, cp, ds_, dr)
    for c in small:
        c.wait()
    total = small_ref[t]
    for i in range(7):
        total = total + small_buf[i]
    both_v[0:16] = total
    both_v[16:32] = cols_ref[...]
    both = [send(both_v, both_buf.at[i], bs.at[i], br.at[i], (p, t)) for i, p in enumerate(others)]
    for c in both:
        c.wait()
    total = both_v[...]
    for i in range(15):
        total = total + both_buf[i]
    cols_out[...] = total[16:32]
    sum_v[...] = total[0:16]
    small_out[t] = total[0:16]
    spread = [send(sum_v, small_out.at[t], gs.at[i], gr.at[i], (d, p)) for i, p in enumerate(tp)]
    own.wait()
    for c in rs:
        c.wait()
    grad_out[...] = stream_back(summed(own_v[...], buf), grad_ref[...], stream_ref[...])
    dp_scatter_finish(copies, mine_v, core_buf, chip_buf, chip, dw_out)
    for c in spread:
        c.wait()


def last_call(part, grad, stream, dw, small, cols, cid):
    rows, width = stream.shape
    wrows, wcols = dw.shape[0] // 16, dw.shape[1]
    dma = pltpu.SemaphoreType.DMA
    return pl.pallas_call(
        last_kernel,
        out_shape=(
            jax.ShapeDtypeStruct(stream.shape, F32),
            jax.ShapeDtypeStruct((wrows, wcols), F32),
            jax.ShapeDtypeStruct((8, 16, 128), F32),
            jax.ShapeDtypeStruct((16, 128), F32),
        ),
        in_specs=[ANY, VM, VM, ANY, VM, VM],
        out_specs=(VM, VM, VM, VM),
        scratch_shapes=[
            pltpu.VMEM((rows, width), BF),
            pltpu.VMEM((7, rows, width), BF),
            pltpu.VMEM((8, wrows, wcols), BF),
            pltpu.VMEM((8, wrows, wcols), BF),
            pltpu.VMEM((7, wrows, wcols), BF),
            pltpu.VMEM((7, 16, 128), F32),
            pltpu.VMEM((32, 128), F32),
            pltpu.VMEM((15, 32, 128), F32),
            pltpu.VMEM((16, 128), F32),
            dma((7,)), dma((7,)), dma((8,)), dma((8,)), dma((2,)),
            dma((7,)), dma((7,)), dma((15,)), dma((15,)), dma((7,)), dma((7,)),
        ],
        compiler_params=pltpu.CompilerParams(
            collective_id=cid, has_side_effects=True, vmem_limit_bytes=32 * 2**20
        ),
        cost_estimate=pl.CostEstimate(flops=0, bytes_accessed=100_000_000, transcendentals=0),
        name="sum_all_gradients",
    )(part, grad, stream, dw.reshape(8, 2, wrows, wcols), small, cols)


def rotate(vectors, cosine, sine_table):
    half_rot = cosine.shape[-1]
    first_rot = vectors[..., :half_rot]
    second = vectors[..., half_rot : 2 * half_rot]
    untouched = vectors[..., 2 * half_rot :]
    return jnp.concatenate(
        [
            first_rot * cosine - second * sine_table,
            second * cosine + first_rot * sine_table,
            untouched,
        ],
        axis=-1,
    )


def positions(lengths, group_rows):
    endings = jnp.cumsum(lengths)
    starts = endings - lengths
    row_ids = jnp.arange(group_rows, dtype=jnp.int32)
    member = (row_ids[:, None] >= starts[None, :]) & (row_ids[:, None] < endings[None, :])
    numbers = jnp.arange(lengths.shape[0], dtype=jnp.int32)
    segment = jnp.sum(jnp.where(member, numbers[None, :], 0), axis=1)
    opening = jnp.sum(jnp.where(member, starts[None, :], 0), axis=1)
    return (segment, row_ids - opening)


def visible(segment, block_start, block_rows):
    group_rows = segment.shape[0]
    query_ids = block_start + jnp.arange(block_rows, dtype=jnp.int32)
    key_ids = jnp.arange(group_rows, dtype=jnp.int32)
    same_doc = segment[block_start : block_start + block_rows][:, None] == segment[None, :]
    return same_doc & (key_ids[None, :] <= query_ids[:, None])


def block_scores(block_queries, keys_rot, segment, block_start, block_rows, score_scale):
    scores = (
        jnp.einsum("bhe,khe->hbk", block_queries, keys_rot, preferred_element_type=F32)
        * score_scale
    )
    return jnp.where(visible(segment, block_start, block_rows)[None], scores, MASKED)


def attend(queries, keys_rot, values_in, segment, block_rows, score_scale):
    outputs = []
    log_totals = []
    for block_start in range(0, queries.shape[0], block_rows):
        block_queries = queries[block_start : block_start + block_rows]
        scores = block_scores(
            block_queries, keys_rot, segment, block_start, block_rows, score_scale
        )
        row_max = jnp.max(scores, axis=-1, keepdims=True)
        exponent = jnp.exp(scores - row_max)
        row_total = jnp.sum(exponent, axis=-1, keepdims=True)
        probability = (exponent / row_total).astype(BF)
        outputs.append(
            jnp.einsum("hbk,khe->bhe", probability, values_in, preferred_element_type=F32)
        )
        log_totals.append(row_max + jnp.log(row_total))
    return (jnp.concatenate(outputs, axis=0), log_totals)


def attend_back(
    queries, keys_rot, values_in, log_totals, attended_grad, segment, block_rows, score_scale
):
    keys_grad = jnp.zeros(keys_rot.shape, F32)
    values_grad = jnp.zeros(values_in.shape, F32)
    query_parts = []
    for block_index, block_start in enumerate(range(0, queries.shape[0], block_rows)):
        block_queries = queries[block_start : block_start + block_rows]
        block_grad = attended_grad[block_start : block_start + block_rows]
        scores = block_scores(
            block_queries, keys_rot, segment, block_start, block_rows, score_scale
        )
        probability = jnp.exp(scores - log_totals[block_index])
        prob_grad = jnp.einsum("bhe,khe->hbk", block_grad, values_in, preferred_element_type=F32)
        centre = jnp.sum(probability * prob_grad, axis=-1, keepdims=True)
        score_grad = (probability * (prob_grad - centre)).astype(BF)
        query_parts.append(
            jnp.einsum("hbk,khe->bhe", score_grad, keys_rot, preferred_element_type=F32)
            * score_scale
        )
        keys_grad = (
            keys_grad
            + jnp.einsum("hbk,bhe->khe", score_grad, block_queries, preferred_element_type=F32)
            * score_scale
        )
        values_grad = values_grad + jnp.einsum(
            "hbk,bhe->khe", probability.astype(BF), block_grad, preferred_element_type=F32
        )
    return (jnp.concatenate(query_parts, axis=0), keys_grad, values_grad)


def nn(a, b):
    return jnp.dot(a, b, preferred_element_type=F32)


def tn(a, b):
    return lax.dot_general(a, b, (((0,), (0,)), ((), ())), preferred_element_type=F32)


def nt(a, b):
    return lax.dot_general(a, b, (((1,), (1,)), ((), ())), preferred_element_type=F32)


def forward(xhat, w, gain, shift, qkv_b, in_b, segment, cosine, sine, block_rows):
    x32 = xhat.astype(F32)
    n1 = (x32 * gain[0] + shift[0]).astype(BF)
    n2 = (x32 * gain[1] + shift[1]).astype(BF)
    proj = nn(n1, w[:, 0:384]) + qkv_b
    rows = xhat.shape[0]
    shape = (rows, 2, HEAD_DIM)
    q = rotate(proj[:, 0:128].reshape(shape), cosine, sine).astype(BF)
    k = rotate(proj[:, 128:256].reshape(shape), cosine, sine).astype(BF)
    v = proj[:, 256:384].reshape(shape).astype(BF)
    attended, logs = attend(q, k, v, segment, block_rows, HEAD_DIM**-0.5)
    attended = attended.reshape(rows, 128).astype(BF)
    pre = nn(n2, w[:, 384:896]) + in_b
    hidden = jax.nn.gelu(pre, approximate=False).astype(BF)
    cat = jnp.concatenate([attended, hidden], axis=1)
    branch = nt(cat, w[:, 896:1536]).astype(BF)
    return branch, (n1, n2, q, k, v, logs, pre, cat)


def backward(grad, xhat, w, gain, kept, segment, cosine, sine, block_rows):
    n1, n2, q, k, v, logs, pre, cat = kept
    rows = xhat.shape[0]
    d_out = tn(grad, cat).astype(BF)
    cat_grad = nn(grad, w[:, 896:1536])
    att_grad = cat_grad[:, 0:128].astype(BF).reshape(q.shape)
    gelu_back = jax.vjp(partial(jax.nn.gelu, approximate=False), pre)[1]
    pre_grad = gelu_back(cat_grad[:, 128:640])[0].astype(BF)
    qg, kg, vg = attend_back(q, k, v, logs, att_grad, segment, block_rows, HEAD_DIM**-0.5)
    proj_grad = jnp.concatenate(
        [
            rotate(qg, cosine, -sine).reshape(rows, 128),
            rotate(kg, cosine, -sine).reshape(rows, 128),
            vg.reshape(rows, 128),
        ],
        axis=1,
    ).astype(BF)
    dw = jnp.concatenate([tn(n1, proj_grad).astype(BF), tn(n2, pre_grad).astype(BF), d_out], axis=1)
    cols = jnp.concatenate(
        [jnp.sum(proj_grad.astype(F32), axis=0), jnp.sum(pre_grad.astype(F32), axis=0)]
    )
    n1_grad = nt(proj_grad, w[:, 0:384])
    n2_grad = nt(pre_grad, w[:, 384:896])
    x32 = xhat.astype(F32)
    small = jnp.stack(
        [
            jnp.sum(n1_grad * x32, axis=0),
            jnp.sum(n2_grad * x32, axis=0),
            jnp.sum(n1_grad, axis=0),
            jnp.sum(n2_grad, axis=0),
        ]
    )
    part = (n1_grad * gain[0] + n2_grad * gain[1]).astype(BF)
    return part, dw, cols, small


def local(
    tokens,
    lengths,
    qkv_weight,
    qkv_bias,
    dense_weight,
    dense_bias,
    fc_in_weight,
    fc_in_bias,
    fc_out_weight,
    fc_out_bias,
    norm_gain,
    norm_bias,
    cotangent,
):
    rows = tokens.shape[0]
    group_rows = rows * 8
    block_rows = 512
    segment, position = positions(lengths[0], group_rows)
    half_rot = ROT // 2
    frequency = 10000.0 ** (-(2.0 * jnp.arange(half_rot, dtype=F32)) / ROT)
    angles = position.astype(F32)[:, None] * frequency[None, :]
    cosine = jnp.cos(angles)[:, None, :]
    sine = jnp.sin(angles)[:, None, :]
    gain = norm_gain.astype(F32)
    shift = norm_bias.astype(F32)
    qkv_b = qkv_bias.astype(F32).reshape(2, 384)
    in_b = fc_in_bias.astype(F32)
    out_b = dense_bias.astype(F32) + fc_out_bias.astype(F32)
    shards = [
        jnp.concatenate(
            [
                qkv_weight[i].reshape(64, 384),
                fc_in_weight[i],
                dense_weight[i].T,
                fc_out_weight[i].T,
            ],
            axis=1,
        )
        for i in range(2)
    ]
    stream0 = tokens.astype(F32)
    xhat0 = normed(stream0)[0].astype(BF)
    grad2 = cotangent.astype(F32)
    grad2_rows = lax.all_gather(cotangent, "tensor", axis=0, tiled=True)

    xg0, w0 = open_call(xhat0, shards[0], 1)
    part, kept0 = forward(xg0, w0, gain[0], shift[0], qkv_b[0], in_b[0], segment, cosine, sine, block_rows)
    stream1, xg1, w1 = middle_call(part, stream0, out_b[0:1], shards[1], 2)
    part, kept1 = forward(xg1, w1, gain[1], shift[1], qkv_b[1], in_b[1], segment, cosine, sine, block_rows)
    branch = lax.psum_scatter(part, "tensor", scatter_dimension=0, tiled=True)
    output = (stream1 + branch.astype(F32) + out_b[1]).astype(BF)

    part, dw1, cols1, small1 = backward(
        grad2_rows, xg1, w1, gain[1], kept1, segment, cosine, sine, block_rows
    )
    grad1, grad1_rows, dw1 = turn_call(part, grad2, stream1, dw1, 3)
    part, dw0, cols0, small0 = backward(
        grad1_rows, xg0, w0, gain[0], kept0, segment, cosine, sine, block_rows
    )
    small = jnp.concatenate(
        [
            small0,
            small1,
            jnp.sum(grad1, axis=0, keepdims=True),
            jnp.sum(grad2, axis=0, keepdims=True),
            jnp.zeros((6, 1024), F32),
        ]
    )
    small = small.reshape(16, 8, 128).swapaxes(0, 1)
    cols = jnp.concatenate([cols0, cols1, jnp.zeros((256,), F32)]).reshape(16, 128)
    input_grad, dw0, small, cols = last_call(part, grad1, stream0, dw0, small, cols, 4)
    small = small.swapaxes(0, 1).reshape(16, 1024)
    cols = cols.reshape(2048)[:1792].reshape(2, 896)
    dw = jnp.stack([dw0, dw1])
    bias_grad = small[8:10]
    norms = small[0:8].reshape(2, 2, 2, 1024)
    return (
        output,
        input_grad,
        dw[:, :, 0:384].reshape(2, 64, 3, 128),
        cols[:, 0:384].reshape(2, 3, 128),
        dw[:, :, 896:1024].swapaxes(1, 2),
        bias_grad,
        dw[:, :, 384:896],
        cols[:, 384:896],
        dw[:, :, 1024:1536].swapaxes(1, 2),
        bias_grad,
        norms[:, 0],
        norms[:, 1],
    )


def solution(mesh):
    return jax.shard_map(
        local,
        mesh=mesh,
        in_specs=(
            P(("dp", "tensor"), None),
            P("dp", None),
            P(None, "dp", None, "tensor"),
            P(None, None, "tensor"),
            P(None, "tensor", "dp"),
            P(),
            P(None, "dp", "tensor"),
            P(None, "tensor"),
            P(None, "tensor", "dp"),
            P(),
            P(),
            P(),
            P(("dp", "tensor"), None),
        ),
        out_specs=(
            P(("dp", "tensor"), None),
            P(("dp", "tensor"), None),
            P(None, "dp", None, "tensor"),
            P(None, None, "tensor"),
            P(None, "tensor", "dp"),
            P(),
            P(None, "dp", "tensor"),
            P(None, "tensor"),
            P(None, "tensor", "dp"),
            P(),
            P(),
            P(),
        ),
        check_vma=False,
    )
```

time: 1540 us -> 459 us (0.30)
  waiting for transfers between devices: 1130 us -> 0.72 us
  Pallas kernels: 0 us -> 255 us
  blocking collectives: 179 us -> 0 us
  matrix products: 133 us -> 96.2 us
  local copies, waits for them, and re-layouts: 21.8 us -> 51 us
    reduce_scatter x14 -> x1, waiting for transfers between devices: 831 us -> 0.01 us  [local(): branch = lax.psum_scatter(part, 'tensor', scatter_dimension=0, tiled=True)]
    all_gather x10 -> x1, waiting for transfers between devices: 291 us -> 0.02 us  [local(): grad2_rows = lax.all_gather(cotangent, 'tensor', axis=0, tiled=True)]
    pallas_call x0 -> x4, Pallas kernels: none -> 255 us  [the longest x1 69.3 us: middle_call(): pl.pallas_call(middle_kernel, out_shape=(jax.ShapeDtypeStruct(stream.shap...]
    psum x2 -> x0, blocking collectives: 94.8 us -> none  [the longest x1 66.3 us: local(): lax.psum((jnp.stack([shared_grads[layer_index][0] for layer_index in rang...]
    all_gather x4 -> x0, blocking collectives: 83.9 us -> none  [the longest x2 48.6 us: fetch_weights(): lax.all_gather(qkv_weight[layer_index], 'dp', axis=0, tiled=True)]
    dot_general x30 -> x26, matrix products: 92.9 us -> 75.5 us  [the longest x6 28.9 us: nn(): return jnp.dot(a, b, preferred_element_type=F32)]
  transfers between devices with their start and end apart: 24 -> 2, of which waited for: 22 -> 0; matrix products, arithmetic and copies ran while one was open for 11% -> 20% of each run, Pallas kernels for 0% -> 41%
where the time goes in v1:
time: 459 us; the launch traced here: 454 us
  Pallas kernels  255 us (56%)
  matrix products  96.2 us (21%)
  local copies, waits for them, and re-layouts  51 us (11%)
  other arithmetic  35.6 us (8%)
  between operations  15.8 us (3%)
    pallas_call x1, Pallas kernels, middle_call(): pl.pallas_call(middle_kernel, out_shape=(jax.ShapeDtypeStruct(stream.shap...  69.3 us
    pallas_call x1, Pallas kernels, turn_call(): pl.pallas_call(turn_kernel, out_shape=(jax.ShapeDtypeStruct(stream.shape,...  67.2 us
    pallas_call x1, Pallas kernels, last_call(): pl.pallas_call(last_kernel, out_shape=(jax.ShapeDtypeStruct(stream.shape,...  60.1 us
    pallas_call x1, Pallas kernels, open_call(): pl.pallas_call(open_kernel, out_shape=(jax.ShapeDtypeStruct((x.shape[0] *...  57.9 us
    dot_general x6, matrix products, nn(): return jnp.dot(a, b, preferred_element_type=F32)  28.9 us
    unnamed x241, local copies, waits for them, and re-layouts  25.3 us
    dot_general x6, matrix products, nt(): lax.dot_general(a, b, (((1,), (1,)), ((), ())), preferred_element_type=F32)  20.1 us
    dot_general x6, matrix products, tn(): lax.dot_general(a, b, (((0,), (0,)), ((), ())), preferred_element_type=F32)  14.7 us
  transfers between devices with their start and end apart: 2, of which 0 were waited for; matrix products, arithmetic and copies ran while one was open for 20% of the time, Pallas kernels for 41%

profile of v1, /device:TPU:1, one launch (start us, length us, event | category | flops | bytes accessed | tf_op | source)
XLA Modules:
  0.0 454.0 jit_solution(14315170223469398263)
XLA Ops:
  17.6 57.9 %gather_weights_and_rows.1 = (bf16[1024,1024]{1,0:T(8,128)(2,1)}, bf16[1024,1536]{1,0:T(8,128)(2,1)}) custom-call(bf16[128,1024]{1,0:T(8,128)(2,1)} %multiply_convert_fusion.6.x_ref, bf16[64,1536]{1,0:T(8,128)(2,1)} %get-tuple-element.182.w_ref), custom_call_target="tpu_custom_call" | custom-call | bytes 80000000 | tf_op jit(solution)/shard_map/gather_weights_and_rows/pallas_call | solution.py:120
  75.5 2.8 fusion.73
  90.3 8.5 %multiply_convert_fusion.5 = (bf16[1024,512]{1,0:T(8,128)(2,1)S(1)}, f32[1024,512]{1,0:T(8,128)}, f32[1024,512]{1,0:T(8,128)}) fusion(f32[512]{0:T(512)S(1)} %bitcast.228, bf16[1024,1536]{1,0:T(8,128)(2,1)} %get-tuple-element.25, bf16[1024,1024]{1,0:T(8,128)(2,1)} %get-tuple-element.24, f32[1024]{0:T(1024)S(1)} %bitcast.246, f32[1024]{0:T(1024)S(1)} %bitcast.243), kind=kOutput, calls=%fused_computation.85 | convolution fusion | flops 1112539136 | bytes 8398848 | tf_op jit(solution)/shard_map/dot_general | solution.py:472
  98.8 3.5 convolution_convert_fusion.1.part_ref
  102.4 69.3 %sum_rows_and_gather.1 = (f32[128,1024]{1,0:T(8,128)S(1)}, bf16[1024,1024]{1,0:T(8,128)(2,1)S(1)}, bf16[1024,1536]{1,0:T(8,128)(2,1)S(1)}) custom-call(bf16[1024,1024]{1,0:T(8,128)(2,1)S(1)} %convolution_convert_fusion.1.part_ref, f32[128,1024]{1,0:T(8,128)S(1)} %convert_element_type.177.stream_ref, f32[1,1024]{1,0:T(1,128)S(1)} %get-tuple-element.142.bias_ref, ...), custom_call_target="tpu_custom_call" | custom-call | bytes 150000000 | tf_op jit(solution)/shard_map/sum_rows_and_gather/pallas_call | solution.py:188
  188.4 5.0 %fusion.179 = (bf16[1024,640]{1,0:T(8,128)(2,1)S(1)}, f32[1024,640]{1,0:T(8,128)}) fusion(bf16[1024,1024]{1,0:T(8,128)(2,1)} %all-gather.2.cloned.1.call-done, bf16[1024,1536]{1,0:T(8,128)(2,1)S(1)} %copy-done.16), kind=kOutput, calls=%fused_computation.319 | convolution fusion | flops 1342832640 | bytes 7340032 | tf_op jit(solution)/shard_map/dot_general | solution.py:472
  195.1 4.0 fusion.24
  199.1 3.7 multiply_reduce_fusion.2
  203.8 3.5 multiply_reduce_fusion.3
  218.7 6.9 %convert_reduce_fusion = (f32[512]{0:T(512)}, bf16[1024,512]{1,0:T(8,128)(2,1)S(1)}, f32[1024,512]{1,0:T(8,128)S(1)}, f32[1024,512]{1,0:T(8,128)S(1)}) fusion(f32[1024,640]{1,0:T(8,128)S(1)} %copy-done.113, f32[512]{0:T(512)S(1)} %bitcast.230, bf16[1024,1536]{1,0:T(8,128)(2,1)S(1)} %copy-done.16, bf16[1024,1024]{1,0:T(8,128)(2,1)S(1)} %copy-done.19, ...), kind=kOutput, calls=%fused_computation.64 | convolution fusion | flops 1117257216 | bytes 10498048 | tf_op jit(solution)/shard_map/dot_general | solution.py:472
  227.8 3.9 fusion.159
  233.3 3.2 convolution_convert_fusion
  236.6 3.6 fusion.72
  242.1 3.2 copy.57
  249.0 67.2 %sum_gradients_and_gather.1 = (f32[128,1024]{1,0:T(8,128)S(1)}, bf16[1024,1024]{1,0:T(8,128)(2,1)S(1)}, f32[64,1536]{1,0:T(8,128)S(1)}) custom-call(bf16[1024,1024]{1,0:T(8,128)(2,1)S(1)} %copy-done.4, f32[128,1024]{1,0:T(8,128)S(1)} %copy-done.10, f32[128,1024]{1,0:T(8,128)S(1)} %copy-done.6, bf16[8,2,64,1536]{3,2,1,0:T(8,128)(2,1)S(1)} %bitcast.165), custom_call_target="tpu_custom_call" | custom-call | bytes 150000000 | tf_op jit(solution)/shard_map/sum_gradients_and_gather/pallas_call | solution.py:275
  316.2 4.6 %fusion.180 = (bf16[1024,640]{0,1:T(8,128)(2,1)S(1)}, f32[1024,640]{0,1:T(8,128)}) fusion(bf16[1024,1024]{1,0:T(8,128)(2,1)S(1)} %get-tuple-element.29, bf16[1024,1536]{1,0:T(8,128)(2,1)} %get-tuple-element.25), kind=kOutput, calls=%fused_computation.320 | convolution fusion | flops 1342832640 | bytes 7340032 | tf_op jit(solution)/shard_map/dot_general | solution.py:472
  331.3 2.7 convolution_convert_fusion.2
  334.1 3.2 fusion.98
  340.9 2.8 fusion.79
  349.8 3.2 copy.59
  354.1 2.8 fusion.127
  357.0 5.2 %fusion.161 = (f32[1024]{0:T(1024)}, f32[1024]{0:T(1024)}, bf16[1024,1024]{1,0:T(8,128)(2,1)}, f32[1024]{0:T(1024)}, f32[1024]{0:T(1024)}) fusion(bf16[1024,1024]{1,0:T(8,128)(2,1)S(1)} %copy-done.111, f32[1024]{0:T(1024)S(1)} %bitcast.245, f32[1024,1024]{1,0:T(8,128)S(1)} %fusion.127, f32[1024]{0:T(1024)S(1)} %bitcast.242, ...), kind=kOutput, calls=%fused_computation.303 | convolution fusion | flops 1085272064 | bytes 10510336 | tf_op jit(solution)/shard_map/dot_general | solution.py:480
  362.8 2.8 concatenate.129
  374.2 60.1 %sum_all_gradients.1 = (f32[128,1024]{1,0:T(8,128)S(1)}, f32[64,1536]{1,0:T(8,128)S(1)}, f32[8,16,128]{2,1,0:T(8,128)S(1)}, f32[16,128]{1,0:T(8,128)S(1)}) custom-call(bf16[1024,1024]{1,0:T(8,128)(2,1)S(1)} %copy-done.11, f32[128,1024]{1,0:T(8,128)S(1)} %copy-done.9, f32[128,1024]{1,0:T(8,128)S(1)} %copy-done.1, bf16[8,2,64,1536]{3,2,1,0:T(8,128)(2,1)S(1)} %bitcast.164, ...), custom_call_target="tpu_custom_call" | custom-call | bytes 100000000 | tf_op jit(solution)/shard_map/sum_all_gradients/pallas_call | solution.py:348
  (367 shorter events, 104.3 us)
Async XLA Ops:
  7.2 8.4 %copy-start.81 = (bf16[2,2,1024]{2,1,0:T(2,128)(2,1)S(1)}, bf16[2,2,1024]{2,1,0:T(2,128)(2,1)}, u32[]{:S(2)}) copy-start(bf16[2,2,1024]{2,1,0:T(2,128)(2,1)} %param.24) | copy-start | bytes 24580
  7.2 9.0 %copy-start.82 = (bf16[2,2,1024]{2,1,0:T(2,128)(2,1)S(1)}, bf16[2,2,1024]{2,1,0:T(2,128)(2,1)}, u32[]{:S(2)}) copy-start(bf16[2,2,1024]{2,1,0:T(2,128)(2,1)} %param.23) | copy-start | bytes 24580
  7.2 9.6 %copy-start.109 = (bf16[2,3,128]{2,0,1:T(2,128)(2,1)S(1)}, bf16[2,3,128]{2,0,1:T(2,128)(2,1)}, u32[]{:S(2)}) copy-start(bf16[2,3,128]{2,0,1:T(2,128)(2,1)} %param.16) | copy-start | bytes 4612
  7.2 181.2 %all-gather.2.cloned.1.call-start = ((), (), s32[]{:S(2)}) async-start(), calls=%async_computation.2 | async-start | bytes 2359296 | tf_op jit(solution)/shard_map/all_gather | solution.py:582
  7.9 435.9 %reduce-scatter.2.cloned.1.call-start = ((), (), s32[]{:S(2)}) async-start(), calls=%async_computation.1 | async-start | bytes 2359296 | tf_op jit(solution)/shard_map/reduce_scatter | solution.py:588
  16.2 62.1 %copy-start.101 = (f32[1,1,1024]{2,1,0:T(1,128)}, f32[1,1,1024]{2,1,0:T(1,128)S(1)}, u32[]{:S(2)}) copy-start(f32[1,1,1024]{2,1,0:T(1,128)S(1)} %get-tuple-element.149) | copy-start | bytes 12292
  16.2 74.1 %copy-start.99 = (f32[1,1,1024]{2,1,0:T(1,128)}, f32[1,1,1024]{2,1,0:T(1,128)S(1)}, u32[]{:S(2)}) copy-start(f32[1,1,1024]{2,1,0:T(1,128)S(1)} %get-tuple-element.150) | copy-start | bytes 12292
  16.2 155.5 %copy-start.107 = (f32[1,1,1024]{2,1,0:T(1,128)}, f32[1,1,1024]{2,1,0:T(1,128)S(1)}, u32[]{:S(2)}) copy-start(f32[1,1,1024]{2,1,0:T(1,128)S(1)} %get-tuple-element.147) | copy-start | bytes 12292
  16.8 61.5 %copy-start.93 = (f32[1,1,1024]{2,1,0:T(1,128)}, f32[1,1,1024]{2,1,0:T(1,128)S(1)}, u32[]{:S(2)}) copy-start(f32[1,1,1024]{2,1,0:T(1,128)S(1)} %get-tuple-element.145) | copy-start | bytes 12292
  16.8 73.5 %copy-start.96 = (f32[1,1,1024]{2,1,0:T(1,128)}, f32[1,1,1024]{2,1,0:T(1,128)S(1)}, u32[]{:S(2)}) copy-start(f32[1,1,1024]{2,1,0:T(1,128)S(1)} %get-tuple-element.146) | copy-start | bytes 12292
  16.8 154.9 %copy-start.103 = (f32[1,1,1024]{2,1,0:T(1,128)}, f32[1,1,1024]{2,1,0:T(1,128)S(1)}, u32[]{:S(2)}) copy-start(f32[1,1,1024]{2,1,0:T(1,128)S(1)} %get-tuple-element.143) | copy-start | bytes 12292
  78.4 9.9 %copy-start.33 = (bf16[1024,128]{0,1:T(8,128)(2,1)}, bf16[1024,128]{0,1:T(8,128)(2,1)S(1)}, u32[]{:S(2)}) copy-start(bf16[1024,128]{0,1:T(8,128)(2,1)S(1)} %slice.640) | copy-start | bytes 786436
  79.3 23.1 %copy-start = (f32[128,1024]{1,0:T(8,128)}, f32[128,1024]{1,0:T(8,128)S(1)}, u32[]{:S(2)}) copy-start(f32[128,1024]{1,0:T(8,128)S(1)} %convert_element_type.177.stream_ref) | copy-start | bytes 1572868
  80.0 10.4 %copy-start.87 = (f32[1,512]{1,0:T(1,128)}, f32[1,512]{1,0:T(1,128)S(1)}, u32[]{:S(2)}) copy-start(f32[1,512]{1,0:T(1,128)S(1)} %get-tuple-element.159) | copy-start | bytes 6148
  81.2 93.3 %copy-start.57 = (f32[1024,8]{0,1:T(8,128)}, f32[1024,8]{0,1:T(8,128)S(1)}, u32[]{:S(2)}) copy-start(f32[1024,8]{0,1:T(8,128)S(1)} %get-tuple-element.153) | copy-start | bytes 98308
  89.6 9.2 %copy-start.75 = (bf16[1024,128]{1,0:T(8,128)(2,1)}, bf16[1024,128]{1,0:T(8,128)(2,1)S(1)}, u32[]{:S(2)}) copy-start(bf16[1024,128]{1,0:T(8,128)(2,1)S(1)} %copy.51) | copy-start | bytes 786436
  181.9 6.4 %copy-start.16 = (bf16[1024,1536]{1,0:T(8,128)(2,1)S(1)}, bf16[1024,1536]{1,0:T(8,128)(2,1)}, u32[]{:S(2)}) copy-start(bf16[1024,1536]{1,0:T(8,128)(2,1)} %copy-done.15) | copy-start | bytes 9437188
  210.7 5.6 %copy-start.31 = (bf16[2,64,1024]{2,1,0:T(8,128)(2,1)}, bf16[2,64,1024]{2,1,0:T(8,128)(2,1)S(1)}, u32[]{:S(2)}) copy-start(bf16[2,64,1024]{2,1,0:T(8,128)(2,1)S(1)} %fusion.95) | copy-start | bytes 786436
  357.0 5.8 %copy-start.85 = (f32[1024]{0:T(1024)S(1)}, f32[1024]{0:T(1024)}, u32[]{:S(2)}) copy-start(f32[1024]{0:T(1024)} %convert_reduce_fusion.5) | copy-start | bytes 12292
  436.5 7.3 %copy-start.7 = (f32[128,1024]{1,0:T(8,128)S(1)}, f32[128,1024]{1,0:T(8,128)}, u32[]{:S(2)}) copy-start(f32[128,1024]{1,0:T(8,128)} %copy-done.5) | copy-start | bytes 1572868
  436.5 7.3 %copy-start.86 = (f32[1,1024]{1,0:T(1,128)S(1)}, f32[1,1024]{1,0:T(1,128)}, u32[]{:S(2)}) copy-start(f32[1,1024]{1,0:T(1,128)} %get-tuple-element.141) | copy-start | bytes 12292
  436.5 5.2 %copy-start.3 = (f32[64,1536]{1,0:T(8,128)S(1)}, f32[64,1536]{1,0:T(8,128)}, u32[]{:S(2)}) copy-start(f32[64,1536]{1,0:T(8,128)} %copy-done.2) | copy-start | bytes 1179652
  438.7 6.9 %copy-start.83 = (f32[2,1024]{1,0:T(2,128)}, f32[2,1024]{1,0:T(2,128)S(1)}, u32[]{:S(2)}) copy-start(f32[2,1024]{1,0:T(2,128)S(1)} %slice_bitcast_fusion.8) | copy-start | bytes 24580
  438.7 7.4 %copy-start.13 = (f32[128,1024]{1,0:T(8,128)S(1)}, f32[128,1024]{1,0:T(8,128)}, u32[]{:S(2)}) copy-start(f32[128,1024]{1,0:T(8,128)} %copy-done.12) | copy-start | bytes 1572868
  (94 other events, 196.0 us)
Sparse Core Ops, SparseCore 0:
  10.4 77.2 all-gather.1
  334.2 79.1 reduce-scatter.1
